TPU v7x, 32 devices: a whole 2x2x4 slice. The times are simulated.
32 devices in a mesh: groups: 2 (over x), lat: 16 (over z, y, core).
Axes of the slice: x: 2, y: 2, z: 4, core: 2. Of those that a mesh axis runs over, the one named last changes fastest.
Arguments:
- spectral: bfloat16 [384, 2, 2, 16, 384], P('lat', None, None, 'groups'), parts along dimension 3, may hold values from -6 to 6
- legendre: bfloat16 [384, 384, 768], P('lat'), may hold values from -0.3125 to 0.3125
- tracers: bfloat16 [768, 30, 16, 1536], P('lat', None, 'groups'), parts along dimension 2, may hold values from 0.19921875 to 2
- rates: float32 [30, 30], replicated, may hold values from -1 to 1
- decay: float32 [30, 8], replicated, may hold values from 0.05 to 2
Outputs:
- tracers_next: bfloat16 [768, 30, 16, 1536], P('lat', None, 'groups'), parts along dimension 2
There are 2 independent parts, one for each index of `groups`. A program takes and returns all parts, laid end to end along the dimension named above; an argument that names none is the same for every part. Nothing has to cross between parts.
All inputs are finite; a program needn't handle non-finite values.
Results may differ from a plain program's by a relative error of at most 0.0029.
Values may be sent and summed in bfloat16 or wider, within the bound.
No kernel may reach another device: no remote copies, remote signals or barrier semaphores. Data moves between devices by JAX's collectives and lax.ppermute only.
A program may use at most 576 MiB of HBM per device.

v0:
```python
import math

import jax
import jax.numpy as jnp
from jax import lax
from jax.sharding import PartitionSpec as P

COURANT = 0.45


def with_halo(value, sides, width):
    for axis, dim in sides:
        devices, length = (lax.axis_size(axis), value.shape[dim])
        up = [(i, (i + 1) % devices) for i in range(devices - 1)]
        down = [(j, i) for i, j in up]
        last = lax.slice_in_dim(value, length - width, length, axis=dim)
        initial = lax.slice_in_dim(value, 0, width, axis=dim)
        before = lax.ppermute(last, axis, up)
        after = lax.ppermute(initial, axis, down)
        value = jnp.concatenate([before, value, after], axis=dim)
    return value


def fourier_basis(wave_total, lon_count):
    wave_ids = lax.broadcasted_iota(jnp.int32, (wave_total, lon_count), 0)
    lon_ids = lax.broadcasted_iota(jnp.int32, (wave_total, lon_count), 1)
    phase = wave_ids * lon_ids % lon_count
    angle = phase.astype(jnp.float32) * (2.0 * math.pi / lon_count)
    factor = 1.0 / math.sqrt(wave_total)
    return jnp.stack([jnp.cos(angle) * factor, -jnp.sin(angle) * factor]).astype(jnp.bfloat16)


def synthesize(received, lon_count):
    basis = fourier_basis(received.shape[0], lon_count)
    return jnp.einsum(
        "mrckl,rmx->lckx", received, basis, preferred_element_type=jnp.float32
    ).astype(jnp.bfloat16)


def limiter(speed):
    return COURANT * speed / (1.0 + jnp.abs(speed))


def advect(q_rows, east_rows, north_rows, rates, decay):
    field = q_rows.astype(jnp.float32)
    east_cells = east_rows.astype(jnp.float32)
    north_cells = north_rows.astype(jnp.float32)
    face_x = limiter(0.5 * (east_cells + jnp.roll(east_cells, -1, axis=2)))[:, None]
    face_y = limiter(0.5 * (north_cells[:-1] + north_cells[1:]))[:, None]
    centre = field[1:-1]
    flux_x = jnp.maximum(face_x, 0.0) * centre + jnp.minimum(face_x, 0.0) * jnp.roll(
        centre, -1, axis=3
    )
    flux_y = jnp.maximum(face_y, 0.0) * field[:-1] + jnp.minimum(face_y, 0.0) * field[1:]
    advected = centre - (flux_x - jnp.roll(flux_x, 1, axis=3)) - (flux_y[1:] - flux_y[:-1])
    coupled = jnp.einsum("ts,lskx->ltkx", rates, advected, precision=lax.Precision.HIGHEST)
    return (jnp.exp(-decay)[None, :, :, None] * advected + coupled).astype(jnp.bfloat16)


def shards(spectral, legendre, tracers, rates, decay):
    wave_count, deg_count, lat_count = legendre.shape
    tracer_count = tracers.shape[1]
    lon_count = tracers.shape[3]
    first_wave = lax.axis_index("lat") * wave_count
    wave_ids = first_wave + lax.broadcasted_iota(jnp.int32, (wave_count, deg_count, 1), 0)
    deg_ids = lax.broadcasted_iota(jnp.int32, (wave_count, deg_count, 1), 1)
    masked = jnp.where(deg_ids >= wave_ids, legendre, jnp.zeros((), jnp.bfloat16))
    fourier = jnp.einsum(
        "mrckn,mnl->mrckl", spectral, masked, preferred_element_type=jnp.float32
    ).astype(jnp.bfloat16)
    received = lax.all_to_all(fourier, "lat", split_axis=4, concat_axis=0, tiled=True)
    winds = synthesize(received, lon_count)
    stacked = jnp.concatenate([tracers, winds[:, 1:2]], axis=1)
    padded = with_halo(stacked, (("lat", 0),), 1)
    q_rows = padded[:, :tracer_count]
    north_rows = padded[:, tracer_count]
    east_rows = winds[:, 0]
    return advect(q_rows, east_rows, north_rows, rates, decay)


def solution(mesh):
    in_specs = (
        P("lat", None, None, "groups", None),
        P("lat", None, None),
        P("lat", None, "groups", None),
        P(),
        P(),
    )
    out_specs = P("lat", None, "groups", None)
    return jax.shard_map(shards, mesh=mesh, in_specs=in_specs, out_specs=out_specs, check_vma=False)
```

profile of v0, /device:TPU:13, one launch (start us, length us, event | category | flops | bytes accessed | tf_op | source)
XLA Modules:
  0.0 752.0 jit_solution(17728058241937306892)
XLA Ops:
  0.0 0.1 iota_compare_fusion
  0.1 1.0 copy-done
  1.1 6.5 fusion.24
  7.6 10.4 %copy.48 = bf16[24,2,2,8,768]{0,3,2,1,4:T(8,128)(2,1)} copy(bf16[24,2,2,8,768]{4,3,2,1,0:T(8,128)(2,1)S(1)} %fusion.24) | data formatting | bytes 2359296 | tf_op jit(solution)/shard_map/convert_element_type | solution.py:70
  18.0 10.4 %reshape.104 = bf16[16,2,18432]{2,1,0:T(2,128)(2,1)} reshape(bf16[768,2,2,8,24]{4,3,2,1,0:T(8,128)(2,1)} %bitcast.63) | data formatting | bytes 2359296
  28.4 6.6 all-to-all-start
  35.0 0.7 copy.47
  35.7 10.6 %multiply_convert_fusion = (bf16[1,384,1536]{2,1,0:T(8,128)(2,1)S(1)}, bf16[1,384,1536]{2,1,0:T(8,128)(2,1)}) fusion(), kind=kLoop, calls=%fused_computation.39 | loop fusion | flops 8257536 | bytes 2359296 | tf_op jit(solution)/shard_map/convert.2
  46.3 16.5 %all-to-all-done = bf16[16,2,18432]{2,1,0:T(2,128)(2,1)S(1)} async-done(((bf16[16,2,18432]{2,1,0:T(2,128)(2,1)}), bf16[16,2,18432]{2,1,0:T(2,128)(2,1)S(1)}, u32[]{:S(2)}, u32[]{:S(2)}) %all-to-all-start) | async-done | bytes 1179680 | tf_op jit(solution)/shard_map/all_to_all | solution.py:71
  62.7 9.7 %reshape.105 = bf16[768,2,2,8,24]{4,3,2,1,0:T(8,128)(2,1)} reshape(bf16[16,2,18432]{2,1,0:T(2,128)(2,1)S(1)} %all-to-all-done) | data formatting | bytes 2359296
  72.4 11.3 %copy.49 = bf16[24,2,2,8,16,48]{5,3,2,1,0,4:T(8,128)(2,1)} copy(bf16[24,2,2,8,16,48]{0,3,2,1,5,4:T(8,128)(2,1)} %bitcast.64) | data formatting | bytes 2359296 | tf_op jit(solution)/shard_map/all_to_all | solution.py:71
  83.7 6.8 copy.58
  90.6 0.0 slice-start.2
  90.6 0.0 slice-start.3
  90.6 0.0 slice-start.4
  90.6 0.0 slice-start.5
  90.6 0.0 slice-start.6
  90.6 0.0 slice-start.8
  90.6 4.7 fusion.12
  95.3 2.7 convert_bitcast_fusion
  98.0 0.3 slice-done.3
  98.3 1.2 slice-done.4
  99.5 1.2 slice-done.5
  100.7 1.2 slice-done.6
  101.9 1.2 slice-done.7
  103.1 0.5 slice-done.8
  103.6 1.3 pad_maximum_fusion.2
  104.9 3.6 collective-permute-start
  108.5 2.2 collective-permute-start.1
  110.7 2.1 slice_bitcast_fusion
  112.8 0.1 copy.52
  112.9 0.2 copy.53
  113.1 5.1 maximum_bitcast_fusion.3
  118.2 0.0 collective-permute-done
  118.2 4.6 collective-permute-done.1
  122.8 25.7 %pad_maximum_fusion = bf16[50,31,8,1536]{3,2,1,0:T(8,128)(2,1)} fusion(bf16[1,31,8,1536]{3,2,1,0:T(8,128)(2,1)S(1)} %collective-permute-done.1, bf16[48,1,8,1536]{3,2,1,0:T(8,128)(2,1)S(1)} %get-tuple-element.12, bf16[48,30,8,1536]{3,2,1,0:T(8,128)(2,1)} %param.7, bf16[1,31,8,1536]{3,2,1,0:T(8,128)(2,1)S(1)} %collective-permute-done), kind=kLoop, calls=%fused_computation.13 | loop fusion | flops 57139200 | bytes 76185600 | tf_op jit(solution)/shard_map/concatenate | solution.py:20
  148.5 36.3 %slice_convert_fusion = f32[50,30,8,1536]{3,2,1,0:T(8,128)} fusion(bf16[50,31,8,1536]{3,2,1,0:T(8,128)(2,1)} %pad_maximum_fusion), kind=kLoop, calls=%fused_computation.14 | loop fusion | flops 18432000 | bytes 110592000 | tf_op jit(solution)/shard_map/convert_element_type | solution.py:45
  184.7 48.0 %slice.92 = f32[48,30,8,1535]{3,2,1,0:T(8,128)} slice(f32[50,30,8,1536]{3,2,1,0:T(8,128)} %slice_convert_fusion), slice={[1:49], [0:30], [0:8], [1:1536]} | slice | bytes 141465600 | tf_op jit(solution)/shard_map/jit(_roll_static)/slice | solution.py:51
  232.8 5.6 slice.93
  238.4 70.4 %fusion.4 = f32[48,30,8,1536]{3,2,1,0:T(8,128)} fusion(f32[48,30,8,1]{3,2,1,0:T(8,128)} %slice.93, f32[48,30,8,1535]{3,2,1,0:T(8,128)} %slice.92, f32[50,30,8,1536]{3,2,1,0:T(8,128)} %slice_convert_fusion, f32[48,8,1536]{2,1,0:T(8,128)} %get-tuple-element.8, f32[48,8,1536]{2,1,0:T(8,128)} %get-tuple-element.7), kind=kLoop, calls=%fused_computation.8 | loop fusion | flops 70778880 | bytes 217055232 | tf_op jit(solution)/shard_map/add | solution.py:51
  308.8 6.9 slice.94
  315.8 0.2 maximum_convert_fusion
  316.0 2.2 maximum_bitcast_fusion
  318.3 71.7 %fusion.2 = f32[49,30,8,1536]{3,2,1,0:T(8,128)} fusion(f32[50,30,8,1536]{3,2,1,0:T(8,128)} %slice_convert_fusion, f32[49,8,1536]{2,1,0:T(8,128)} %get-tuple-element.10, f32[49,8,1536]{2,1,0:T(8,128)S(1)} %get-tuple-element.9), kind=kLoop, calls=%fused_computation.3 | loop fusion | flops 54190080 | bytes 221577216 | tf_op jit(solution)/shard_map/add | solution.py:54
  390.0 131.9 %fusion.3 = f32[48,30,8,1536]{3,2,1,0:T(8,128)} fusion(f32[49,30,8,1536]{3,2,1,0:T(8,128)} %fusion.2, f32[48,30,8,1536]{3,2,1,0:T(8,128)} %fusion.4, f32[48,30,8,1535]{3,2,1,0:T(8,128)} %bitcast.60, f32[48,30,8,1]{3,2,1,0:T(8,128)} %slice.94, f32[50,30,8,1536]{3,2,1,0:T(8,128)} %slice_convert_fusion), kind=kLoop, calls=%fused_computation.6 | loop fusion | flops 88473600 | bytes 424673280 | tf_op jit(solution)/shard_map/sub | solution.py:55
  521.9 165.6 %fusion = f32[48,8,1536,30]{2,3,1,0:T(8,128)} fusion(f32[48,30,8,1536]{3,2,1,0:T(8,128)} %fusion.3, f32[30,30]{1,0:T(8,128)S(1)} %copy-done.4), kind=kOutput, calls=%fused_computation | convolution fusion | flops 6370099200 | bytes 141561360 | tf_op jit(solution)/shard_map/ts,lskx->ltkx/dot_general | solution.py:56
  687.6 0.0 copy-start.1
  687.6 64.2 %fusion.6 = bf16[48,30,8,1536]{3,2,1,0:T(8,128)(2,1)} fusion(f32[48,8,1536,30]{2,3,1,0:T(8,128)} %fusion, f32[48,30,8,1536]{3,2,1,0:T(8,128)} %fusion.3, f32[30,8]{1,0:T(8,128)S(1)} %copy-done.3), kind=kLoop, calls=%fused_computation.12 | loop fusion | flops 53084160 | bytes 176948160 | tf_op jit(solution)/shard_map/convert_element_type | solution.py:57
  (20 shorter events, 0.1 us)
Async XLA Ops:
  0.0 1.1 copy-start
  18.0 16.9 %copy-start.5 = (f32[30,8]{0,1:T(8,128)S(1)}, f32[30,8]{0,1:T(8,128)}, u32[]{:S(2)}) copy-start(f32[30,8]{0,1:T(8,128)} %param.9) | copy-start | bytes 2884
  28.4 34.3 %all-to-all-start = ((bf16[16,2,18432]{2,1,0:T(2,128)(2,1)}), bf16[16,2,18432]{2,1,0:T(2,128)(2,1)S(1)}, u32[]{:S(2)}, u32[]{:S(2)}) async-start(bf16[16,2,18432]{2,1,0:T(2,128)(2,1)} %reshape.104), calls=%async_computation | async-start | bytes 2359296 | tf_op jit(solution)/shard_map/all_to_all | solution.py:71
  83.7 6.8 copy-start.2
  90.6 7.4 slice-start
  90.6 7.5 slice-start.1
  90.6 7.5 slice-start.2
  90.6 7.8 %slice-start.3 = ((s8[35389440]{0:T(1024)(128)(4,1)}), s8[4194304]{0:T(1024)(128)(4,1)S(1)}, s32[]{:S(2)}) async-start(s8[35389440]{0:T(1024)(128)(4,1)} %bitcast.61), calls=%async_computation.4 | async-start | bytes 8388608
  90.6 8.9 %slice-start.4 = ((s8[35389440]{0:T(1024)(128)(4,1)}), s8[4194304]{0:T(1024)(128)(4,1)S(1)}, s32[]{:S(2)}) async-start(s8[35389440]{0:T(1024)(128)(4,1)} %bitcast.61), calls=%async_computation.5 | async-start | bytes 8388608
  90.6 10.1 %slice-start.5 = ((s8[35389440]{0:T(1024)(128)(4,1)}), s8[4194304]{0:T(1024)(128)(4,1)S(1)}, s32[]{:S(2)}) async-start(s8[35389440]{0:T(1024)(128)(4,1)} %bitcast.61), calls=%async_computation.6 | async-start | bytes 8388608
  90.6 11.3 %slice-start.6 = ((s8[35389440]{0:T(1024)(128)(4,1)}), s8[4194304]{0:T(1024)(128)(4,1)S(1)}, s32[]{:S(2)}) async-start(s8[35389440]{0:T(1024)(128)(4,1)} %bitcast.61), calls=%async_computation.7 | async-start | bytes 8388608
  90.6 12.5 %slice-start.7 = ((s8[35389440]{0:T(1024)(128)(4,1)}), s8[4194304]{0:T(1024)(128)(4,1)S(1)}, s32[]{:S(2)}) async-start(s8[35389440]{0:T(1024)(128)(4,1)} %bitcast.61), calls=%async_computation.8 | async-start | bytes 8388608
  90.6 13.0 %slice-start.8 = ((s8[35389440]{0:T(1024)(128)(4,1)}), s8[1835008]{0:T(1024)(128)(4,1)S(1)}, s32[]{:S(2)}) async-start(s8[35389440]{0:T(1024)(128)(4,1)} %bitcast.61), calls=%async_computation.9 | async-start | bytes 3670016
  104.9 13.3 %collective-permute-start = (bf16[1,31,8,1536]{3,2,1,0:T(8,128)(2,1)}, bf16[1,31,8,1536]{3,2,1,0:T(8,128)(2,1)S(1)}, u32[]{:S(2)}, u32[]{:S(2)}) collective-permute-start(bf16[1,31,8,1536]{3,2,1,0:T(8,128)(2,1)} %get-tuple-element.5), channel_id=1, source_target_pairs={{0,1},{1,2},{2,3},{3,4},{4,5},{5,6},{6,7},{7,8},{8,9},{9,10},{10,1... | collective-permute-start | bytes 2285576 | tf_op jit(solution)/shard_map/ppermute | solution.py:18
  108.5 14.3 %collective-permute-start.1 = (bf16[1,31,8,1536]{3,2,1,0:T(8,128)(2,1)}, bf16[1,31,8,1536]{3,2,1,0:T(8,128)(2,1)S(1)}, u32[]{:S(2)}, u32[]{:S(2)}) collective-permute-start(bf16[1,31,8,1536]{3,2,1,0:T(8,128)(2,1)} %get-tuple-element.6), channel_id=1, source_target_pairs={{1,0},{2,1},{3,2},{4,3},{5,4},{6,5},{7,6},{8,7},{9,8},{10,9},{11,1... | collective-permute-start | bytes 2285576 | tf_op jit(solution)/shard_map/ppermute | solution.py:19
  390.0 131.9 %copy-start.4 = (f32[30,30]{1,0:T(8,128)S(1)}, f32[30,30]{1,0:T(8,128)}, u32[]{:S(2)}) copy-start(f32[30,30]{1,0:T(8,128)} %param.8) | copy-start | bytes 10804
  521.9 165.7 %copy-start.3 = (f32[30,8]{1,0:T(8,128)S(1)}, f32[30,8]{1,0:T(8,128)}, u32[]{:S(2)}) copy-start(f32[30,8]{1,0:T(8,128)} %copy.47) | copy-start | bytes 2884
  687.6 64.2 %copy-start.1 = (bf16[24,2,2,8,384]{4,3,2,1,0:T(8,128)(2,1)S(1)}, bf16[24,2,2,8,384]{4,3,2,1,0:T(8,128)(2,1)}, u32[]{:S(2)}) copy-start(bf16[24,2,2,8,384]{4,3,2,1,0:T(8,128)(2,1)} %param.5) | copy-start | bytes 1769476
where the time goes:
time: 759 us; the launch traced here: 752 us
  other arithmetic  422 us (56%)
  matrix products  177 us (23%)
  local copies, waits for them, and re-layouts  119 us (16%)
  waiting for transfers between devices  21 us (3%)
  starting transfers between devices  12.3 us (2%)
    dot_general x1, matrix products, advect(): jnp.einsum('ts,lskx->ltkx', rates, advected, precision=lax.Precision.HIGH...  166 us
    sub x1, other arithmetic, advect(): centre - (flux_x - jnp.roll(flux_x, 1, axis=3)) - (flux_y[1:] - flux_y[:-1])  132 us
    add x1, other arithmetic, advect(): jnp.maximum(face_y, 0.0) * field[:-1] + jnp.minimum(face_y, 0.0) * field[1:]  71.7 us
    add x1, other arithmetic, advect(): jnp.maximum(face_x, 0.0) * centre  70.4 us
    convert_element_type x1, other arithmetic, advect(): (jnp.exp(-decay)[None, :, :, None] * advected + coupled).astype(jnp.bfloa...  64.2 us
    slice x2, local copies, waits for them, and re-layouts, advect(): jnp.roll(centre, -1, axis=3)  53.7 us
    convert_element_type x1, other arithmetic, advect(): field = q_rows.astype(jnp.float32)  36.3 us
    unnamed x32, local copies, waits for them, and re-layouts  26.7 us
  transfers between devices with their start and end apart: 3, of which 2 were waited for; matrix products, arithmetic and copies ran while one was open for 2% of the time, Pallas kernels for 0%

commit v1 on v0

v1 whole, which is shorter than its diff:
```python
import functools
import math

import jax
import jax.numpy as jnp
from jax import lax
from jax.experimental import pallas as pl
from jax.experimental.pallas import tpu as pltpu
from jax.sharding import PartitionSpec as P

COURANT = 0.45
BF = jnp.bfloat16
F32 = jnp.float32
LANES = 128
VMEM_LIMIT = 56 * 2**20


def divisor(count, most):
    return max(d for d in range(1, most + 1) if count % d == 0)


def tiles(ref, first, count):
    return jnp.concatenate([ref[j, pl.ds(first, count), :] for j in range(ref.shape[0])], axis=1)


def params():
    return pltpu.CompilerParams(vmem_limit_bytes=VMEM_LIMIT)


def legendre_kernel(waves, first_ref, spec_ref, leg_ref, out_ref, four_ref):
    step = pl.program_id(0)
    per_step, _, _, levels, degs = spec_ref.shape
    lats = leg_ref.shape[2]
    lines = spec_ref.shape[1] * spec_ref.shape[2] * levels
    deg = lax.broadcasted_iota(jnp.int32, (lines, degs), 1)
    for i in range(per_step):
        wave = step * per_step + i
        coeffs = spec_ref[i].astype(F32).reshape(lines, degs)
        coeffs = jnp.where(deg >= first_ref[0] + wave, coeffs, 0.0).astype(BF)
        res = jnp.dot(coeffs, leg_ref[i], preferred_element_type=F32)
        for j in range(lats // LANES):
            four_ref[j, pl.ds(wave, lines, stride=waves), :] = res[:, j * LANES : (j + 1) * LANES]

    @pl.when(step == pl.num_programs(0) - 1)
    def _():
        dests = out_ref.shape[0]
        rows = lats // dests
        half = lines // 2
        for ck in range(half):
            both = jnp.concatenate(
                [
                    tiles(four_ref, first, waves)
                    for first in (ck * waves, (half + ck) * waves)
                ],
                axis=0,
            ).astype(BF)
            for d in range(dests):
                out_ref[d, :, ck * rows : (ck + 1) * rows] = both[:, d * rows : (d + 1) * rows]


def legendre_synthesis(first, spectral, legendre, dests):
    waves, parts, comps, levels, degs = spectral.shape
    lats = legendre.shape[2]
    per_step = divisor(waves, 4)
    rows = lats // dests
    lines = parts * comps * levels
    return pl.pallas_call(
        functools.partial(legendre_kernel, waves),
        grid=(waves // per_step,),
        in_specs=[
            pl.BlockSpec(memory_space=pltpu.SMEM),
            pl.BlockSpec((per_step, parts, comps, levels, degs), lambda i: (i, 0, 0, 0, 0)),
            pl.BlockSpec((per_step, degs, lats), lambda i: (i, 0, 0)),
        ],
        out_specs=pl.BlockSpec((dests, parts * waves, comps * levels * rows), lambda i: (0, 0, 0)),
        out_shape=jax.ShapeDtypeStruct((dests, parts * waves, comps * levels * rows), BF),
        scratch_shapes=[pltpu.VMEM((lats // LANES, lines * waves, LANES), F32)],
        compiler_params=params(),
        cost_estimate=pl.CostEstimate(
            flops=2 * lines * waves * degs * lats,
            bytes_accessed=2 * (legendre.size + 2 * spectral.size),
            transcendentals=0,
        ),
        name="legendre",
    )(first, spectral, legendre)


def tables_kernel(waves, wave_total, rates_ref, decay_ref, basis_ref, weight_ref):
    rows, lons = basis_ref.shape
    tracers, levels = decay_ref.shape
    both = tracers * levels
    lanes = LANES
    factor = 1.0 / math.sqrt(wave_total)
    chunk = divisor(rows, 96)

    def body(i, _):
        start = pl.multiple_of(i * chunk, chunk)
        row = start + lax.broadcasted_iota(jnp.int32, (chunk, lanes), 0)
        lon = lax.broadcasted_iota(jnp.int32, (chunk, lanes), 1)
        wave = row // (2 * waves) * waves + row % waves
        imag = row // waves % 2 == 1
        unit = 2.0 * math.pi / lons
        phase = (wave * lon % lons).astype(F32) * unit
        turn = (wave * lanes % lons).astype(F32) * unit
        c, s = jnp.cos(phase) * factor, jnp.sin(phase) * factor
        tc, ts = jnp.cos(turn), jnp.sin(turn)
        for j in range(lons // lanes):
            basis_ref[pl.ds(start, chunk), j * lanes : (j + 1) * lanes] = jnp.where(
                imag, -s, c
            ).astype(BF)
            c, s = c * tc - s * ts, s * tc + c * ts
        return 0

    lax.fori_loop(0, rows // chunk, body, 0)
    spread = (
        lax.broadcasted_iota(jnp.int32, (both, tracers), 0) // levels
        == lax.broadcasted_iota(jnp.int32, (both, tracers), 1)
    ).astype(F32)
    high = functools.partial(
        lax.dot_general, precision=lax.Precision.HIGHEST, preferred_element_type=F32
    )
    rows_of = high(spread, rates_ref[...], (((1,), (0,)), ((), ())))
    full = high(rows_of, spread, (((1,), (1,)), ((), ())))
    kept = high(spread, jnp.exp(-decay_ref[...]), (((1,), (0,)), ((), ())))
    own = lax.broadcasted_iota(jnp.int32, (both, levels), 0) % levels == lax.broadcasted_iota(
        jnp.int32, (both, levels), 1
    )
    kept = jnp.sum(jnp.where(own, kept, 0.0), axis=1, keepdims=True)
    row = lax.broadcasted_iota(jnp.int32, (both, both), 0)
    col = lax.broadcasted_iota(jnp.int32, (both, both), 1)
    full = jnp.where(row % levels == col % levels, full, 0.0)
    full = full + jnp.where(row == col, kept, 0.0)
    weight_ref[0] = full.astype(BF)
    weight_ref[1] = (full - full.astype(BF).astype(F32)).astype(BF)


def tables(rates, decay, waves, wave_total, lons):
    both = decay.shape[0] * decay.shape[1]
    return pl.pallas_call(
        functools.partial(tables_kernel, waves, wave_total),
        out_shape=(
            jax.ShapeDtypeStruct((2 * wave_total, lons), BF),
            jax.ShapeDtypeStruct((2, both, both), BF),
        ),
        compiler_params=params(),
        cost_estimate=pl.CostEstimate(
            flops=2 * wave_total * lons * 40, bytes_accessed=4 * wave_total * lons, transcendentals=0
        ),
        name="tables",
    )(rates, decay)


def winds_kernel(levels, rows, four_ref, basis_ref, winds_ref):
    cols = 256
    turned = four_ref[...].T
    comps = four_ref.shape[1] // (levels * rows)
    for j in range(basis_ref.shape[1] // cols):
        span = pl.ds(j * cols, cols)
        res = jnp.dot(turned, basis_ref[:, span], preferred_element_type=F32)
        res = res.astype(BF).astype(F32)
        for c in range(comps):
            for k in range(levels):
                first = (c * levels + k) * rows
                for h in range(cols // LANES):
                    tile = j * cols // LANES + h
                    winds_ref[tile, pl.ds(c * rows * levels + k, rows, stride=levels), :] = res[
                        first : first + rows, h * LANES : (h + 1) * LANES
                    ]


def wind_synthesis(received, basis, levels, rows):
    count = received.shape[1]
    return pl.pallas_call(
        functools.partial(winds_kernel, levels, rows),
        out_shape=jax.ShapeDtypeStruct((basis.shape[1] // LANES, count, LANES), F32),
        compiler_params=params(),
        cost_estimate=pl.CostEstimate(
            flops=2 * basis.size * count,
            bytes_accessed=2 * (basis.size + received.size) + 4 * count * basis.shape[1],
            transcendentals=0,
        ),
        name="winds",
    )(received, basis)


def limiter(speed):
    return COURANT * speed / (1.0 + jnp.abs(speed))


def twice(value):
    return jnp.concatenate([value, value], axis=0).astype(BF)


def advect_kernel(
    levels, weight_ref, q_ref, qn_ref, before_ref, after_ref, east_ref, north_ref, nb_ref, na_ref,
    out_ref, flux_ref, next_ref, gain_a, gain_b,
):
    step = pl.program_id(0)
    last = pl.num_programs(0) - 1
    rows, both, lons = q_ref.shape
    zero = jnp.zeros((), BF)
    pairs = [slice(s, s + 2 * levels) for s in range(0, both, 2 * levels)]

    @pl.when(step == 0)
    def _():
        face = twice(limiter(0.5 * (tiles(nb_ref, 0, levels) + tiles(north_ref, 0, levels))))
        for p in pairs:
            flux_ref[p] = face * jnp.where(face > zero, before_ref[0, p], q_ref[0, p])

    @pl.when(step == last)
    def _():
        next_ref[...] = after_ref[0]

    @pl.when(step != last)
    def _():
        next_ref[...] = qn_ref[0]

    lat = step * rows
    total = north_ref.shape[1] // levels
    gains = [gain_a, gain_b]
    for r in range(rows + 1):
        if r < rows:
            east = tiles(east_ref, r * levels, levels)
            face = limiter(0.5 * (east + pltpu.roll(east, lons - 1, 1)))
            cx, cw = twice(face), twice(pltpu.roll(face, 1, 1))
            here = tiles(north_ref, pl.multiple_of((lat + r) * levels, levels), levels)
            if r < rows - 1:
                there = tiles(north_ref, pl.multiple_of((lat + r + 1) * levels, levels), levels)
            else:
                inside = jnp.minimum(lat + r + 1, total - 1)
                there = tiles(north_ref, pl.multiple_of(inside * levels, levels), levels)
                there = jnp.where(step == last, tiles(na_ref, 0, levels), there)
            cy = twice(limiter(0.5 * (here + there)))
            mx, mw, my = cx > zero, cw > zero, cy > zero
            for p in pairs:
                q0 = q_ref[r, p]
                q1 = q_ref[r + 1, p] if r < rows - 1 else next_ref[p]
                fx = cx * jnp.where(mx, q0, pltpu.roll(q0, lons - 1, 1))
                fw = cw * jnp.where(mw, pltpu.roll(q0, 1, 1), q0)
                fy = cy * jnp.where(my, q0, q1)
                gains[r % 2][p] = (fw - fx) + (flux_ref[p] - fy)
                flux_ref[p] = fy
        if r > 0:
            q0, gain = q_ref[r - 1], gains[(r - 1) % 2][...]
            out_ref[r - 1] = (
                jnp.dot(weight_ref[0], q0, preferred_element_type=F32)
                + jnp.dot(weight_ref[1], q0, preferred_element_type=F32)
                + jnp.dot(weight_ref[0], gain, preferred_element_type=F32)
            ).astype(BF)


def advect(weight, q, before, after, winds, north_before, north_after, levels):
    total, both, lons = q.shape
    rows = divisor(total, 6)
    whole = lambda *shape: pl.BlockSpec(shape, lambda i: (0,) * len(shape))
    return pl.pallas_call(
        functools.partial(advect_kernel, levels),
        grid=(total // rows,),
        in_specs=[
            whole(2, both, both),
            pl.BlockSpec((rows, both, lons), lambda i: (i, 0, 0)),
            pl.BlockSpec((1, both, lons), lambda i: (jnp.minimum(rows * (i + 1), total - 1), 0, 0)),
            whole(1, both, lons),
            whole(1, both, lons),
            pl.BlockSpec((lons // LANES, rows * levels, LANES), lambda i: (0, i, 0)),
            pl.BlockSpec((lons // LANES, total * levels, LANES), lambda i: (0, 1, 0)),
            whole(lons // LANES, levels, LANES),
            whole(lons // LANES, levels, LANES),
        ],
        out_specs=pl.BlockSpec((rows, both, lons), lambda i: (i, 0, 0)),
        out_shape=jax.ShapeDtypeStruct(q.shape, BF),
        scratch_shapes=[pltpu.VMEM((both, lons), BF)] * 4,
        compiler_params=params(),
        cost_estimate=pl.CostEstimate(
            flops=2 * both * q.size, bytes_accessed=5 * q.size, transcendentals=0
        ),
        name="advect",
    )(weight, q, q, before, after, winds, winds, north_before, north_after)


def shards(spectral, legendre, tracers, rates, decay):
    waves, _, comps, levels, _ = spectral.shape
    rows, tracer_count, _, lons = tracers.shape
    devices = lax.axis_size("lat")
    me = lax.axis_index("lat")
    up = [(i, i + 1) for i in range(devices - 1)]
    down = [(j, i) for i, j in up]
    q = tracers.reshape(rows, tracer_count * levels, lons)
    before = lax.ppermute(q[-1:], "lat", up)
    after = lax.ppermute(q[:1], "lat", down)
    first = jnp.full((1,), me * waves, jnp.int32)
    fourier = legendre_synthesis(first, spectral, legendre, devices)
    before, after, fourier = lax.optimization_barrier((before, after, fourier))
    received = lax.all_to_all(fourier, "lat", split_axis=0, concat_axis=0, tiled=True)
    basis, weight = tables(rates, decay, waves, waves * devices, lons)
    received = received.reshape(devices * 2 * waves, comps * levels * rows)
    winds = wind_synthesis(received, basis, levels, rows)
    north_before = lax.ppermute(winds[:, -levels:], "lat", up)
    north_after = lax.ppermute(winds[:, rows * levels : (rows + 1) * levels], "lat", down)
    out = advect(weight, q, before, after, winds, north_before, north_after, levels)
    return out.reshape(tracers.shape)


def solution(mesh):
    in_specs = (
        P("lat", None, None, "groups", None),
        P("lat", None, None),
        P("lat", None, "groups", None),
        P(),
        P(),
    )
    out_specs = P("lat", None, "groups", None)
    return jax.shard_map(shards, mesh=mesh, in_specs=in_specs, out_specs=out_specs, check_vma=False)
```

time: 759 us -> 115 us (0.15)
  other arithmetic: 422 us -> 0 us
  matrix products: 177 us -> 0 us
  local copies, waits for them, and re-layouts: 119 us -> 4.63 us
  Pallas kernels: 0 us -> 65.1 us
  starting transfers between devices: 12.3 us -> 23.2 us
    dot_general x3 -> x0, matrix products: 177 us -> none  [the longest x1 166 us: advect(): jnp.einsum('ts,lskx->ltkx', rates, advected, precision=lax.Precision.HIGH...]
    add x3 -> x0, other arithmetic: 142 us -> none  [the longest x1 71.7 us: advect(): jnp.maximum(face_y, 0.0) * field[:-1] + jnp.minimum(face_y, 0.0) * field[1:]]
    sub x1 -> x0, other arithmetic: 132 us -> none  [advect(): centre - (flux_x - jnp.roll(flux_x, 1, axis=3)) - (flux_y[1:] - flux_y[:-1])]
    convert_element_type x4 -> x0, other arithmetic: 103 us -> none  [the longest x1 64.2 us: advect(): (jnp.exp(-decay)[None, :, :, None] * advected + coupled).astype(jnp.bfloa...]
    pallas_call x0 -> x4, Pallas kernels: none -> 65.1 us  [the longest x1 40.2 us: advect(): pl.pallas_call(functools.partial(advect_kernel, levels), grid=(total // r...]
    slice x5 -> x2, local copies, waits for them, and re-layouts: 60.8 us -> 2.26 us  [the longest x1 1.43 us: shards(): after = lax.ppermute(q[:1], 'lat', down)]
    concatenate x1 -> x0, other arithmetic: 25.7 us -> none  [with_halo(): value = jnp.concatenate([before, value, after], axis=dim)]
    unnamed x32 -> x13, local copies, waits for them, and re-layouts: 26.7 us -> 2.36 us
  transfers between devices with their start and end apart: 3 -> 5, of which waited for: 2 -> 2; matrix products, arithmetic and copies ran while one was open for 2% -> 1% of each run, Pallas kernels for 0% -> 16%
where the time goes in v1:
time: 115 us; the launch traced here: 114 us
  Pallas kernels  65.1 us (57%)
  starting transfers between devices  23.2 us (20%)
  waiting for transfers between devices  20.6 us (18%)
  local copies, waits for them, and re-layouts  4.63 us (4%)
    pallas_call x1, Pallas kernels, advect(): pl.pallas_call(functools.partial(advect_kernel, levels), grid=(total // r...  40.2 us
    all_to_all x1, waiting for transfers between devices, shards(): lax.all_to_all(fourier, 'lat', split_axis=0, concat_axis=0, tiled=True)  19.5 us
    pallas_call x1, Pallas kernels, legendre_synthesis(): pl.pallas_call(functools.partial(legendre_kernel, waves), grid=(waves //...  10.4 us
    all_to_all x1, starting transfers between devices, shards(): lax.all_to_all(fourier, 'lat', split_axis=0, concat_axis=0, tiled=True)  10.3 us
    pallas_call x1, Pallas kernels, tables(): pl.pallas_call(functools.partial(tables_kernel, waves, wave_total), out_s...  7.59 us
    pallas_call x1, Pallas kernels, wind_synthesis(): pl.pallas_call(functools.partial(winds_kernel, levels, rows), out_shape=j...  6.91 us
    ppermute x1, starting transfers between devices, shards(): north_before = lax.ppermute(winds[:, -levels:], 'lat', up)  4.34 us
    ppermute x1, starting transfers between devices, shards(): before = lax.ppermute(q[-1:], 'lat', up)  3.88 us
  transfers between devices with their start and end apart: 5, of which 2 were waited for; matrix products, arithmetic and copies ran while one was open for 1% of the time, Pallas kernels for 16%

profile of v1, /device:TPU:13, one launch (start us, length us, event | category | flops | bytes accessed | tf_op | source)
XLA Modules:
  0.0 113.6 jit_solution(3968153843283286086)
XLA Ops:
  0.0 1.4 %slice_bitcast_fusion = (bf16[1,240,1536]{2,1,0:T(8,128)(2,1)S(1)}, bf16[1,240,1536]{2,1,0:T(8,128)(2,1)S(1)}) fusion(bf16[48,30,8,1536]{3,2,1,0:T(8,128)(2,1)} %param.7), kind=kLoop, calls=%fused_computation | loop fusion | bytes 2949120 | tf_op jit(solution)/shard_map/slice | solution.py:290
  1.4 2.6 %collective-permute-start.1 = (bf16[1,240,1536]{2,1,0:T(8,128)(2,1)S(1)}, bf16[1,240,1536]{2,1,0:T(8,128)(2,1)S(1)}, u32[]{:S(2)}, u32[]{:S(2)}) collective-permute-start(bf16[1,240,1536]{2,1,0:T(8,128)(2,1)S(1)} %get-tuple-element.15), channel_id=1, source_target_pairs={{1,0},{2,1},{3,2},{4,3},{5,4},{6,5},{7,6},{8,7},{9,8},{10,9},{11,1... | collective-permute-start | bytes 2211848 | tf_op jit(solution)/shard_map/ppermute | solution.py:290
  4.0 3.9 %collective-permute-start = (bf16[1,240,1536]{2,1,0:T(8,128)(2,1)S(1)}, bf16[1,240,1536]{2,1,0:T(8,128)(2,1)S(1)}, u32[]{:S(2)}, u32[]{:S(2)}) collective-permute-start(bf16[1,240,1536]{2,1,0:T(8,128)(2,1)S(1)} %get-tuple-element.16), channel_id=1, source_target_pairs={{0,1},{1,2},{2,3},{3,4},{4,5},{5,6},{6,7},{7,8},{8,9},{9,10},{10,1... | collective-permute-start | bytes 2211848 | tf_op jit(solution)/shard_map/ppermute | solution.py:289
  7.9 0.0 copy-start.5
  7.9 10.4 %legendre.1 = bf16[16,48,768]{2,1,0:T(8,128)(2,1)} custom-call(s32[1]{0:T(128)} %bitcast.3.first_ref, bf16[24,2,2,8,384]{4,3,2,1,0:T(8,128)(2,1)} %spec_ref.1, bf16[24,384,768]{2,1,0:T(8,128)(2,1)} %leg_ref.1), custom_call_target="tpu_custom_call" | custom-call | flops 452984832 | bytes 15335424 | tf_op jit(solution)/shard_map/legendre/pallas_call | solution.py:67
  18.3 0.0 collective-permute-done.1.after_ref
  18.3 0.0 copy-start.1
  18.3 0.0 collective-permute-done.before_ref
  18.3 0.0 copy-start.2
  18.3 10.3 %all-to-all-start = ((bf16[16,48,768]{2,1,0:T(8,128)(2,1)}), bf16[16,48,768]{2,1,0:T(8,128)(2,1)S(1)}, u32[]{:S(2)}, u32[]{:S(2)}) async-start(bf16[16,48,768]{2,1,0:T(8,128)(2,1)} %legendre.1), calls=%async_computation | async-start | bytes 2359296 | tf_op jit(solution)/shard_map/all_to_all | solution.py:294
  28.6 0.0 copy-done.5
  28.6 0.7 copy.6.decay_ref
  29.3 7.6 %tables.1 = (bf16[768,1536]{1,0:T(8,128)(2,1)}, bf16[2,240,240]{2,1,0:T(8,128)(2,1)}) custom-call(f32[30,30]{1,0:T(8,128)} %rates_ref.1, f32[30,8]{1,0:T(8,128)} %copy.6.decay_ref), custom_call_target="tpu_custom_call" | custom-call | flops 47185920 | bytes 2359296 | tf_op jit(solution)/shard_map/tables/pallas_call | solution.py:139
  36.9 19.5 %all-to-all-done = bf16[16,48,768]{2,1,0:T(8,128)(2,1)S(1)} async-done(((bf16[16,48,768]{2,1,0:T(8,128)(2,1)}), bf16[16,48,768]{2,1,0:T(8,128)(2,1)S(1)}, u32[]{:S(2)}, u32[]{:S(2)}) %all-to-all-start) | async-done | bytes 1179680 | tf_op jit(solution)/shard_map/all_to_all | solution.py:294
  56.3 0.0 copy-start
  56.3 1.0 copy-done
  57.4 6.9 %winds.1.east_ref.north_ref = f32[12,768,128]{2,1,0:T(8,128)} custom-call(bf16[768,768]{1,0:T(8,128)(2,1)} %bitcast.10, bf16[768,1536]{1,0:T(8,128)(2,1)} %get-tuple-element.14.basis_ref), custom_call_target="tpu_custom_call" | custom-call | flops 1811939328 | bytes 8257536 | tf_op jit(solution)/shard_map/winds/pallas_call | solution.py:173
  64.3 0.0 copy-done.1
  64.3 0.0 copy-done.2
  64.3 0.8 fusion
  65.1 2.1 %collective-permute-start.3 = (f32[12,8,128]{2,1,0:T(8,128)S(1)}, f32[12,8,128]{2,1,0:T(8,128)S(1)}, u32[]{:S(2)}, u32[]{:S(2)}) collective-permute-start(f32[12,8,128]{2,1,0:T(8,128)S(1)} %get-tuple-element.17), channel_id=1, source_target_pairs={{1,0},{2,1},{3,2},{4,3},{5,4},{6,5},{7,6},{8,7},{9,8},{10,9},{11,1... | collective-permute-start | bytes 147464 | tf_op jit(solution)/shard_map/ppermute | solution.py:299
  67.3 4.3 %collective-permute-start.2 = (f32[12,8,128]{2,1,0:T(8,128)S(1)}, f32[12,8,128]{2,1,0:T(8,128)S(1)}, u32[]{:S(2)}, u32[]{:S(2)}) collective-permute-start(f32[12,8,128]{2,1,0:T(8,128)S(1)} %get-tuple-element.18), channel_id=1, source_target_pairs={{0,1},{1,2},{2,3},{3,4},{4,5},{5,6},{6,7},{7,8},{8,9},{9,10},{10,1... | collective-permute-start | bytes 147464 | tf_op jit(solution)/shard_map/ppermute | solution.py:298
  71.6 0.0 collective-permute-done.3.na_ref
  71.6 0.0 copy-start.3
  71.6 1.1 collective-permute-done.2.nb_ref
  72.8 0.0 copy-start.4
  72.8 0.0 copy-done.3
  72.8 0.6 copy-done.4
  73.4 40.2 %advect.1 = bf16[48,240,1536]{2,1,0:T(8,128)(2,1)} custom-call(bf16[2,240,240]{2,1,0:T(8,128)(2,1)} %get-tuple-element.10.weight_ref, bf16[48,240,1536]{2,1,0:T(8,128)(2,1)} %bitcast.8, bf16[48,240,1536]{2,1,0:T(8,128)(2,1)} %bitcast.9, bf16[1,240,1536]{2,1,0:T(8,128)(2,1)} %copy-done.2, bf16[1,240,1536]{2,1,0:T(8,128)(2,1)} %copy-done.1, ...), custom_call_target="tpu_custom_call" | custom-call | flops 8493465600 | bytes 88473600 | tf_op jit(solution)/shard_map/advect/pallas_call | solution.py:256
Async XLA Ops:
  1.4 16.9 %collective-permute-start.1 = (bf16[1,240,1536]{2,1,0:T(8,128)(2,1)S(1)}, bf16[1,240,1536]{2,1,0:T(8,128)(2,1)S(1)}, u32[]{:S(2)}, u32[]{:S(2)}) collective-permute-start(bf16[1,240,1536]{2,1,0:T(8,128)(2,1)S(1)} %get-tuple-element.15), channel_id=1, source_target_pairs={{1,0},{2,1},{3,2},{4,3},{5,4},{6,5},{7,6},{8,7},{9,8},{10,9},{11,1... | collective-permute-start | bytes 2211848 | tf_op jit(solution)/shard_map/ppermute | solution.py:290
  4.0 14.3 %collective-permute-start = (bf16[1,240,1536]{2,1,0:T(8,128)(2,1)S(1)}, bf16[1,240,1536]{2,1,0:T(8,128)(2,1)S(1)}, u32[]{:S(2)}, u32[]{:S(2)}) collective-permute-start(bf16[1,240,1536]{2,1,0:T(8,128)(2,1)S(1)} %get-tuple-element.16), channel_id=1, source_target_pairs={{0,1},{1,2},{2,3},{3,4},{4,5},{5,6},{6,7},{7,8},{8,9},{9,10},{10,1... | collective-permute-start | bytes 2211848 | tf_op jit(solution)/shard_map/ppermute | solution.py:289
  7.9 20.7 %copy-start.5 = (f32[30,8]{0,1:T(8,128)S(1)}, f32[30,8]{0,1:T(8,128)}, u32[]{:S(2)}) copy-start(f32[30,8]{0,1:T(8,128)} %param.9) | copy-start | bytes 2884
  18.3 46.0 %copy-start.1 = (bf16[1,240,1536]{2,1,0:T(8,128)(2,1)}, bf16[1,240,1536]{2,1,0:T(8,128)(2,1)S(1)}, u32[]{:S(2)}) copy-start(bf16[1,240,1536]{2,1,0:T(8,128)(2,1)S(1)} %collective-permute-done.1.after_ref) | copy-start | bytes 2211844
  18.3 46.0 %copy-start.2 = (bf16[1,240,1536]{2,1,0:T(8,128)(2,1)}, bf16[1,240,1536]{2,1,0:T(8,128)(2,1)S(1)}, u32[]{:S(2)}) copy-start(bf16[1,240,1536]{2,1,0:T(8,128)(2,1)S(1)} %collective-permute-done.before_ref) | copy-start | bytes 2211844
  18.3 38.0 %all-to-all-start = ((bf16[16,48,768]{2,1,0:T(8,128)(2,1)}), bf16[16,48,768]{2,1,0:T(8,128)(2,1)S(1)}, u32[]{:S(2)}, u32[]{:S(2)}) async-start(bf16[16,48,768]{2,1,0:T(8,128)(2,1)} %legendre.1), calls=%async_computation | async-start | bytes 2359296 | tf_op jit(solution)/shard_map/all_to_all | solution.py:294
  56.3 1.0 copy-start
  65.1 6.5 %collective-permute-start.3 = (f32[12,8,128]{2,1,0:T(8,128)S(1)}, f32[12,8,128]{2,1,0:T(8,128)S(1)}, u32[]{:S(2)}, u32[]{:S(2)}) collective-permute-start(f32[12,8,128]{2,1,0:T(8,128)S(1)} %get-tuple-element.17), channel_id=1, source_target_pairs={{1,0},{2,1},{3,2},{4,3},{5,4},{6,5},{7,6},{8,7},{9,8},{10,9},{11,1... | collective-permute-start | bytes 147464 | tf_op jit(solution)/shard_map/ppermute | solution.py:299
  67.3 5.5 %collective-permute-start.2 = (f32[12,8,128]{2,1,0:T(8,128)S(1)}, f32[12,8,128]{2,1,0:T(8,128)S(1)}, u32[]{:S(2)}, u32[]{:S(2)}) collective-permute-start(f32[12,8,128]{2,1,0:T(8,128)S(1)} %get-tuple-element.18), channel_id=1, source_target_pairs={{0,1},{1,2},{2,3},{3,4},{4,5},{5,6},{6,7},{7,8},{8,9},{9,10},{10,1... | collective-permute-start | bytes 147464 | tf_op jit(solution)/shard_map/ppermute | solution.py:298
  71.6 1.1 %copy-start.3 = (f32[12,8,128]{2,1,0:T(8,128)}, f32[12,8,128]{2,1,0:T(8,128)S(1)}, u32[]{:S(2)}) copy-start(f32[12,8,128]{2,1,0:T(8,128)S(1)} %collective-permute-done.3.na_ref) | copy-start | bytes 147460
  72.8 0.6 copy-start.4

commit v2 on v1

v2 whole, which is shorter than its diff:
```python
import functools
import math

import jax
import jax.numpy as jnp
from jax import lax
from jax.experimental import pallas as pl
from jax.experimental.pallas import tpu as pltpu
from jax.sharding import PartitionSpec as P

COURANT = 0.45
BF = jnp.bfloat16
F32 = jnp.float32
LANES = 128


def divisor(count, most):
    return max(d for d in range(1, most + 1) if count % d == 0)


def tiles(ref, first, count):
    return jnp.concatenate([ref[j, pl.ds(first, count), :] for j in range(ref.shape[0])], axis=1)


def wave_group(waves):
    return divisor(waves, 8)


def params(mebibytes):
    return pltpu.CompilerParams(vmem_limit_bytes=mebibytes * 2**20)


def legendre_kernel(windows, rows, first_ref, spec_ref, leg_ref, *refs):
    *out_refs, four_ref = refs
    step = pl.program_id(0)
    group, _, _, levels, degs = spec_ref.shape
    lats = leg_ref.shape[2]
    lines = spec_ref.shape[1] * spec_ref.shape[2] * levels
    deg = lax.broadcasted_iota(jnp.int32, (lines, degs), 1)
    for i in range(group):
        coeffs = spec_ref[i].astype(F32).reshape(lines, degs)
        coeffs = jnp.where(deg >= first_ref[0] + step * group + i, coeffs, 0.0).astype(BF)
        res = jnp.dot(coeffs, leg_ref[i], preferred_element_type=F32)
        for j in range(lats // LANES):
            four_ref[j, pl.ds(i, lines, stride=group), :] = res[:, j * LANES : (j + 1) * LANES]
    half = lines // 2
    for ck in range(half):
        both = jnp.concatenate(
            [tiles(four_ref, first, group) for first in (ck * group, (half + ck) * group)], axis=0
        ).astype(BF)
        for (begin, width), out_ref in zip(windows, out_refs):
            for d in range(lats // rows):
                low, high = d * rows + begin, d * rows + begin + width
                inside = both[:, max(low, 0) : min(high, lats)]
                if low < 0 or high > lats:
                    out_ref[d, :, ck * width : (ck + 1) * width] = jnp.zeros((2 * group, width), BF)
                lane = ck * width + max(-low, 0)
                out_ref[d, :, lane : lane + inside.shape[1]] = inside


def legendre_synthesis(first, spectral, legendre, windows, rows):
    waves, parts, comps, levels, degs = spectral.shape
    lats = legendre.shape[2]
    dests = lats // rows
    group = wave_group(waves)
    lines = parts * comps * levels
    widths = [comps * levels * width for _, width in windows]
    return pl.pallas_call(
        functools.partial(legendre_kernel, windows, rows),
        grid=(waves // group,),
        in_specs=[
            pl.BlockSpec(memory_space=pltpu.SMEM),
            pl.BlockSpec((group, parts, comps, levels, degs), lambda i: (i, 0, 0, 0, 0)),
            pl.BlockSpec((group, degs, lats), lambda i: (i, 0, 0)),
        ],
        out_specs=[pl.BlockSpec((dests, parts * group, w), lambda i: (0, i, 0)) for w in widths],
        out_shape=[jax.ShapeDtypeStruct((dests, parts * waves, w), BF) for w in widths],
        scratch_shapes=[pltpu.VMEM((lats // LANES, lines * group, LANES), F32)],
        compiler_params=params(56),
        cost_estimate=pl.CostEstimate(
            flops=2 * lines * waves * degs * lats,
            bytes_accessed=2 * (legendre.size + 2 * spectral.size),
            transcendentals=0,
        ),
        name="legendre",
    )(first, spectral, legendre)


def tables_kernel(waves, wave_total, rates_ref, decay_ref, basis_ref, weight_ref):
    rows, lons = basis_ref.shape
    tracers, levels = decay_ref.shape
    both = tracers * levels
    lanes = LANES
    factor = 1.0 / math.sqrt(wave_total)
    chunk = divisor(rows, 96)

    def body(i, _):
        start = pl.multiple_of(i * chunk, chunk)
        row = start + lax.broadcasted_iota(jnp.int32, (chunk, lanes), 0)
        lon = lax.broadcasted_iota(jnp.int32, (chunk, lanes), 1)
        group = wave_group(waves)
        wave = row // (2 * group) * group + row % group
        imag = row // group % 2 == 1
        unit = 2.0 * math.pi / lons
        phase = (wave * lon % lons).astype(F32) * unit
        turn = (wave * lanes % lons).astype(F32) * unit
        c, s = jnp.cos(phase) * factor, jnp.sin(phase) * factor
        tc, ts = jnp.cos(turn), jnp.sin(turn)
        for j in range(lons // lanes):
            basis_ref[pl.ds(start, chunk), j * lanes : (j + 1) * lanes] = jnp.where(
                imag, -s, c
            ).astype(BF)
            c, s = c * tc - s * ts, s * tc + c * ts
        return 0

    lax.fori_loop(0, rows // chunk, body, 0)
    spread = (
        lax.broadcasted_iota(jnp.int32, (both, tracers), 0) // levels
        == lax.broadcasted_iota(jnp.int32, (both, tracers), 1)
    ).astype(F32)
    high = functools.partial(
        lax.dot_general, precision=lax.Precision.HIGHEST, preferred_element_type=F32
    )
    rows_of = high(spread, rates_ref[...], (((1,), (0,)), ((), ())))
    full = high(rows_of, spread, (((1,), (1,)), ((), ())))
    kept = high(spread, jnp.exp(-decay_ref[...]), (((1,), (0,)), ((), ())))
    own = lax.broadcasted_iota(jnp.int32, (both, levels), 0) % levels == lax.broadcasted_iota(
        jnp.int32, (both, levels), 1
    )
    kept = jnp.sum(jnp.where(own, kept, 0.0), axis=1, keepdims=True)
    row = lax.broadcasted_iota(jnp.int32, (both, both), 0)
    col = lax.broadcasted_iota(jnp.int32, (both, both), 1)
    full = jnp.where(row % levels == col % levels, full, 0.0)
    full = full + jnp.where(row == col, kept, 0.0)
    weight_ref[0] = full.astype(BF)
    weight_ref[1] = (full - full.astype(BF).astype(F32)).astype(BF)


def tables(rates, decay, waves, wave_total, lons):
    both = decay.shape[0] * decay.shape[1]
    return pl.pallas_call(
        functools.partial(tables_kernel, waves, wave_total),
        out_shape=(
            jax.ShapeDtypeStruct((2 * wave_total, lons), BF),
            jax.ShapeDtypeStruct((2, both, both), BF),
        ),
        compiler_params=params(56),
        cost_estimate=pl.CostEstimate(
            flops=2 * wave_total * lons * 40, bytes_accessed=4 * wave_total * lons, transcendentals=0
        ),
        name="tables",
    )(rates, decay)


def limiter(speed):
    return COURANT * speed / (1.0 + jnp.abs(speed))


def twice(value):
    return jnp.concatenate([value, value], axis=0).astype(BF)


def synthesize(levels, four_ref, basis_ref, turned_ref, east_ref, north_ref):
    turned_ref[...] = four_ref[...].T
    rows = east_ref.shape[1] // levels
    cols = 2
    for j in range(east_ref.shape[0] // cols):
        span = slice(j * cols * LANES, (j + 1) * cols * LANES)
        res = jnp.dot(turned_ref[...], basis_ref[:, span], preferred_element_type=F32)
        res = res.astype(BF).astype(F32)
        for h in range(cols):
            tile = res[:, h * LANES : (h + 1) * LANES]
            for c, ref in enumerate((east_ref, north_ref)):
                for k in range(levels):
                    first = (c * levels + k) * rows
                    ref[j * cols + h, pl.ds(k, rows, stride=levels), :] = tile[first : first + rows]


def advect_kernel(levels, first, begin, ends, weight_ref, q_ref, qn_ref, prev_ref, *refs):
    after_refs, refs = (refs[:1], refs[1:]) if ends else ((), refs)
    four_ref, basis_ref, *refs = refs
    out_ref, flux_ref, next_ref, gain_a, gain_b, turned_ref, east_ref, north_ref = refs[-8:]
    step = pl.program_id(0)
    rows, both, lons = q_ref.shape
    zero = jnp.zeros((), BF)
    pairs = [slice(s, s + 2 * levels) for s in range(0, both, 2 * levels)]

    def wind(ref, row):
        start = (step * rows + first + row - begin) * levels
        return tiles(ref, pl.multiple_of(start, levels), levels)

    @pl.when(step == 0)
    def _():
        synthesize(levels, four_ref, basis_ref, turned_ref, east_ref, north_ref)
        face = twice(limiter(0.5 * (wind(north_ref, -1) + wind(north_ref, 0))))
        for p in pairs:
            flux_ref[p] = face * jnp.where(face > zero, prev_ref[0, p], q_ref[0, p])

    if ends:
        last = pl.num_programs(0) - 1

        @pl.when(step == last)
        def _():
            next_ref[...] = after_refs[0][0]

        @pl.when(step != last)
        def _():
            next_ref[...] = qn_ref[0]

    gains = [gain_a, gain_b]
    for r in range(rows + 1):
        if r < rows:
            east = wind(east_ref, r)
            face = limiter(0.5 * (east + pltpu.roll(east, lons - 1, 1)))
            cx, cw = twice(face), twice(pltpu.roll(face, 1, 1))
            cy = twice(limiter(0.5 * (wind(north_ref, r) + wind(north_ref, r + 1))))
            mx, mw, my = cx > zero, cw > zero, cy > zero
            for p in pairs:
                q0 = q_ref[r, p]
                if r < rows - 1:
                    q1 = q_ref[r + 1, p]
                else:
                    q1 = next_ref[p] if ends else qn_ref[0, p]
                fx = cx * jnp.where(mx, q0, pltpu.roll(q0, lons - 1, 1))
                fw = cw * jnp.where(mw, pltpu.roll(q0, 1, 1), q0)
                fy = cy * jnp.where(my, q0, q1)
                gains[r % 2][p] = (fw - fx) + (flux_ref[p] - fy)
                flux_ref[p] = fy
        if r > 0:
            q0, gain = q_ref[r - 1], gains[(r - 1) % 2][...]
            out_ref[r - 1] = (
                jnp.dot(weight_ref[0], q0, preferred_element_type=F32)
                + jnp.dot(weight_ref[1], q0, preferred_element_type=F32)
                + jnp.dot(weight_ref[0], gain, preferred_element_type=F32)
            ).astype(BF)


def advect(weight, q, prev, after, fourier, basis, levels, rows, first, count, begin, done):
    total, both, lons = q.shape
    base = first // rows
    ends = first + rows * count == total
    whole = lambda *shape: pl.BlockSpec(
        shape, lambda i: (0,) * len(shape), pipeline_mode=pl.Buffered(1)
    )
    winds = pltpu.VMEM((lons // LANES, fourier.shape[1] // 2, LANES), F32)
    one = lambda index: pl.BlockSpec((1, both, lons), lambda i: (index(i), 0, 0))
    operands = [weight, q, q, prev if first == 0 else q, *[after] * ends, fourier, basis]
    in_specs = [
        whole(2, both, both),
        pl.BlockSpec((rows, both, lons), lambda i: (i + base, 0, 0)),
        one(lambda i: jnp.minimum(rows * (i + base + 1), total - 1)),
        pl.BlockSpec(
            (1, both, lons), lambda i: (max(first - 1, 0), 0, 0), pipeline_mode=pl.Buffered(1)
        ),
        *[whole(1, both, lons)] * ends,
        whole(*fourier.shape),
        whole(*basis.shape),
    ]
    aliases = {}
    if done is not None:
        aliases = {len(operands): 0}
        operands.append(done)
        in_specs.append(pl.BlockSpec(memory_space=pl.ANY))
    return pl.pallas_call(
        functools.partial(advect_kernel, levels, first, begin, ends),
        grid=(count,),
        in_specs=in_specs,
        out_specs=pl.BlockSpec((rows, both, lons), lambda i: (i + base, 0, 0)),
        out_shape=jax.ShapeDtypeStruct(q.shape, BF),
        scratch_shapes=[pltpu.VMEM((both, lons), BF)] * 4
        + [pltpu.VMEM(fourier.shape[::-1], BF), winds, winds],
        input_output_aliases=aliases,
        compiler_params=params(56),
        cost_estimate=pl.CostEstimate(
            flops=6 * both * rows * count * both * lons,
            bytes_accessed=5 * rows * count * both * lons,
            transcendentals=0,
        ),
        name="advect",
    )(*operands)


def exchange(value):
    devices, lines, width = value.shape
    received = lax.all_to_all(value, "lat", split_axis=0, concat_axis=0, tiled=True)
    return received.reshape(devices * lines, width)


def shards(spectral, legendre, tracers, rates, decay):
    waves, _, comps, levels, _ = spectral.shape
    rows, tracer_count, _, lons = tracers.shape
    devices = lax.axis_size("lat")
    up = [(i, i + 1) for i in range(devices - 1)]
    down = [(j, i) for i, j in up]
    per_step = divisor(rows, 6)
    blocks = rows // per_step
    counts = [blocks] if blocks < 4 else [blocks * 3 // 8, blocks - blocks * 3 // 8]
    firsts = [per_step * sum(counts[:i]) for i in range(len(counts))]
    windows = []
    for start, count in zip(firsts, counts):
        width = pl.cdiv(per_step * count + 2, 8) * 8
        windows.append((min(start - 1, rows + 1 - width) if start > 0 else -1, width))
    q = tracers.reshape(rows, tracer_count * levels, lons)
    before, after = lax.ppermute(q[-1:], "lat", up), lax.ppermute(q[:1], "lat", down)
    first = jnp.full((1,), lax.axis_index("lat") * waves, jnp.int32)
    sent = list(legendre_synthesis(first, spectral, legendre, windows, rows))
    basis, weight = tables(rates, decay, waves, waves * devices, lons)
    received = []
    for i in range(len(sent)):
        if i > 0:
            received[-1], sent[i], weight = lax.optimization_barrier((received[-1], sent[i], weight))
        received.append(exchange(sent[i]))
    done = None
    for fourier, start, count, (begin, _) in zip(received, firsts, counts, windows):
        done = advect(
            weight, q, before, after, fourier, basis, levels, per_step, start, count, begin, done
        )
    return done.reshape(tracers.shape)


def solution(mesh):
    in_specs = (
        P("lat", None, None, "groups", None),
        P("lat", None, None),
        P("lat", None, "groups", None),
        P(),
        P(),
    )
    out_specs = P("lat", None, "groups", None)
    return jax.shard_map(shards, mesh=mesh, in_specs=in_specs, out_specs=out_specs, check_vma=False)
```

time: 115 us -> 94.6 us (0.82)
  waiting for transfers between devices: 20.6 us -> 4.49 us
  starting transfers between devices: 23.2 us -> 17 us
  Pallas kernels: 65.1 us -> 66.6 us
  local copies, waits for them, and re-layouts: 4.63 us -> 5.89 us
    all_to_all x1 -> x2, waiting for transfers between devices: 19.5 us -> 0.48 us  [exchange(): lax.all_to_all(value, 'lat', split_axis=0, concat_axis=0, tiled=True)]
    ppermute x4 -> x2, starting transfers between devices: 12.9 us -> 5.76 us  [the longest x1 3.33 us: shards(): lax.ppermute(q[-1:], 'lat', up)]
    ppermute x4 -> x2, waiting for transfers between devices: 1.14 us -> 4.01 us  [the longest x1 4.01 us: shards(): lax.ppermute(q[:1], 'lat', down)]
    pallas_call x3, Pallas kernels: 57.5 us -> 59.1 us  [the longest x2 49.1 us: advect(): pl.pallas_call(functools.partial(advect_kernel, levels, first, begin, end...]
    all_to_all x1 -> x2, starting transfers between devices: 10.3 us -> 11.2 us  [exchange(): lax.all_to_all(value, 'lat', split_axis=0, concat_axis=0, tiled=True)]
    unnamed x13 -> x9, local copies, waits for them, and re-layouts: 2.36 us -> 3.35 us
    slice x2 -> x1, local copies, waits for them, and re-layouts: 2.26 us -> 2.55 us  [shards(): q[-1:]]
  transfers between devices with their start and end apart: 5 -> 4, of which waited for: 2 -> 2; matrix products, arithmetic and copies ran while one was open for 1% -> 4% of each run, Pallas kernels for 16% -> 29%
where the time goes in v2:
time: 94.6 us; the launch traced here: 94.1 us
  Pallas kernels  66.6 us (70%)
  starting transfers between devices  17 us (18%)
  local copies, waits for them, and re-layouts  5.89 us (6%)
  waiting for transfers between devices  4.49 us (5%)
    pallas_call x2, Pallas kernels, advect(): pl.pallas_call(functools.partial(advect_kernel, levels, first, begin, end...  49.1 us
    all_to_all x2, starting transfers between devices, exchange(): lax.all_to_all(value, 'lat', split_axis=0, concat_axis=0, tiled=True)  11.2 us
    pallas_call x1, Pallas kernels, legendre_synthesis(): pl.pallas_call(functools.partial(legendre_kernel, windows, rows), grid=(w...  9.98 us
    pallas_call x1, Pallas kernels, tables(): pl.pallas_call(functools.partial(tables_kernel, waves, wave_total), out_s...  7.59 us
    ppermute x1, waiting for transfers between devices, shards(): lax.ppermute(q[:1], 'lat', down)  4.01 us
    unnamed x9, local copies, waits for them, and re-layouts  3.35 us
    ppermute x1, starting transfers between devices, shards(): lax.ppermute(q[-1:], 'lat', up)  3.33 us
    slice x1, local copies, waits for them, and re-layouts, shards(): q[-1:]  2.55 us
  transfers between devices with their start and end apart: 4, of which 2 were waited for; matrix products, arithmetic and copies ran while one was open for 4% of the time, Pallas kernels for 29%

profile of v2, /device:TPU:13, one launch (start us, length us, event | category | flops | bytes accessed | tf_op | source)
XLA Modules:
  0.0 94.1 jit_solution(11509432240679389135)
XLA Ops:
  0.0 10.0 %legendre.1 = (bf16[16,48,384]{2,1,0:T(8,128)(2,1)}, bf16[16,48,512]{2,1,0:T(8,128)(2,1)}) custom-call(s32[1]{0:T(128)} %bitcast.first_ref, bf16[24,2,2,8,384]{4,3,2,1,0:T(8,128)(2,1)} %spec_ref.1, bf16[24,384,768]{2,1,0:T(8,128)(2,1)} %leg_ref.1), custom_call_target="tpu_custom_call" | custom-call | flops 452984832 | bytes 15335424 | tf_op jit(solution)/shard_map/legendre/pallas_call | solution.py:68
  10.0 6.6 %all-to-all-start = ((bf16[16,48,384]{2,1,0:T(8,128)(2,1)}), bf16[16,48,384]{2,1,0:T(8,128)(2,1)S(1)}, u32[]{:S(2)}, u32[]{:S(2)}) async-start(bf16[16,48,384]{2,1,0:T(8,128)(2,1)} %get-tuple-element.12), calls=%async_computation | async-start | bytes 1179648 | tf_op jit(solution)/shard_map/all_to_all | solution.py:285
  16.5 2.5 %slice_bitcast_fusion = (bf16[1,240,1536]{2,1,0:T(8,128)(2,1)}, bf16[1,240,1536]{2,1,0:T(8,128)(2,1)}) fusion(bf16[48,30,8,1536]{3,2,1,0:T(8,128)(2,1)} %param.7), kind=kLoop, calls=%fused_computation | loop fusion | bytes 2949120 | tf_op jit(solution)/shard_map/slice | solution.py:304
  19.1 3.3 %collective-permute-start.1 = (bf16[1,240,1536]{2,1,0:T(8,128)(2,1)}, bf16[1,240,1536]{2,1,0:T(8,128)(2,1)S(1)}, u32[]{:S(2)}, u32[]{:S(2)}) collective-permute-start(bf16[1,240,1536]{2,1,0:T(8,128)(2,1)} %get-tuple-element.19), channel_id=1, source_target_pairs={{0,1},{1,2},{2,3},{3,4},{4,5},{5,6},{6,7},{7,8},{8,9},{9,10},{10,1... | collective-permute-start | bytes 2211848 | tf_op jit(solution)/shard_map/ppermute | solution.py:304
  22.4 1.4 %copy.7.decay_ref = f32[30,8]{1,0:T(8,128)} copy(f32[30,8]{0,1:T(8,128)} %param.9) | data formatting | bytes 1920 | tf_op args[4]
  23.8 7.6 %tables.1 = (bf16[768,1536]{1,0:T(8,128)(2,1)}, bf16[2,240,240]{2,1,0:T(8,128)(2,1)}) custom-call(f32[30,30]{1,0:T(8,128)} %rates_ref.1, f32[30,8]{1,0:T(8,128)} %copy.7.decay_ref), custom_call_target="tpu_custom_call" | custom-call | flops 47185920 | bytes 2359296 | tf_op jit(solution)/shard_map/tables/pallas_call | solution.py:141
  31.4 0.5 all-to-all-done
  31.9 0.0 copy-start.1
  31.9 4.7 %all-to-all-start.1 = ((bf16[16,48,512]{2,1,0:T(8,128)(2,1)}), bf16[16,48,512]{2,1,0:T(8,128)(2,1)S(1)}, u32[]{:S(2)}, u32[]{:S(2)}) async-start(bf16[16,48,512]{2,1,0:T(8,128)(2,1)} %get-tuple-element.16), calls=%async_computation.1 | async-start | bytes 1572864 | tf_op jit(solution)/shard_map/all_to_all | solution.py:285
  36.5 2.4 %collective-permute-start = (bf16[1,240,1536]{2,1,0:T(8,128)(2,1)}, bf16[1,240,1536]{2,1,0:T(8,128)(2,1)S(1)}, u32[]{:S(2)}, u32[]{:S(2)}) collective-permute-start(bf16[1,240,1536]{2,1,0:T(8,128)(2,1)} %get-tuple-element.20), channel_id=1, source_target_pairs={{1,0},{2,1},{3,2},{4,3},{5,4},{6,5},{7,6},{8,7},{9,8},{10,9},{11,1... | collective-permute-start | bytes 2211848 | tf_op jit(solution)/shard_map/ppermute | solution.py:304
  39.0 0.0 collective-permute-done.1.prev_ref
  39.0 0.0 copy-start.2
  39.0 0.0 copy-done.1
  39.0 0.9 copy-done.2
  39.9 19.8 %advect.2.refs_3_ = bf16[48,240,1536]{2,1,0:T(8,128)(2,1)} custom-call(bf16[2,240,240]{2,1,0:T(8,128)(2,1)} %get-tuple-element.15.weight_ref, bf16[48,240,1536]{2,1,0:T(8,128)(2,1)} %bitcast.9, bf16[48,240,1536]{2,1,0:T(8,128)(2,1)} %bitcast.10, bf16[1,240,1536]{2,1,0:T(8,128)(2,1)} %copy-done.2, bf16[768,384]{1,0:T(8,128)(2,1)} %bitcast.15, ...), custom_call_target="tpu_custom_call" | custom-call | flops 9555148800 | bytes 33177600 | tf_op jit(solution)/shard_map/advect/pallas_call | solution.py:264
  59.7 4.0 %collective-permute-done.refs_0_ = bf16[1,240,1536]{2,1,0:T(8,128)(2,1)S(1)} collective-permute-done((bf16[1,240,1536]{2,1,0:T(8,128)(2,1)}, bf16[1,240,1536]{2,1,0:T(8,128)(2,1)S(1)}, u32[]{:S(2)}, u32[]{:S(2)}) %collective-permute-start) | collective-permute-done | bytes 737312 | tf_op jit(solution)/shard_map/ppermute | solution.py:304
  63.7 0.0 copy-start.3
  63.7 0.0 all-to-all-done.1
  63.7 0.0 copy-start
  63.7 0.9 copy-done.3
  64.6 0.2 copy-done
  64.9 29.2 %advect.3 = bf16[48,240,1536]{2,1,0:T(8,128)(2,1)} custom-call(bf16[2,240,240]{2,1,0:T(8,128)(2,1)} %get-tuple-element.15.weight_ref, bf16[48,240,1536]{2,1,0:T(8,128)(2,1)} %bitcast.11, bf16[48,240,1536]{2,1,0:T(8,128)(2,1)} %bitcast.12, bf16[48,240,1536]{2,1,0:T(8,128)(2,1)} %bitcast.13, ...), custom_call_target="tpu_custom_call", output_to_operand_aliasing={{}: (7, {})} | custom-call | flops 15925248000 | bytes 55296000 | tf_op jit(solution)/shard_map/advect/pallas_call | solution.py:264
Async XLA Ops:
  10.0 21.9 %all-to-all-start = ((bf16[16,48,384]{2,1,0:T(8,128)(2,1)}), bf16[16,48,384]{2,1,0:T(8,128)(2,1)S(1)}, u32[]{:S(2)}, u32[]{:S(2)}) async-start(bf16[16,48,384]{2,1,0:T(8,128)(2,1)} %get-tuple-element.12), calls=%async_computation | async-start | bytes 1179648 | tf_op jit(solution)/shard_map/all_to_all | solution.py:285
  19.1 19.9 %collective-permute-start.1 = (bf16[1,240,1536]{2,1,0:T(8,128)(2,1)}, bf16[1,240,1536]{2,1,0:T(8,128)(2,1)S(1)}, u32[]{:S(2)}, u32[]{:S(2)}) collective-permute-start(bf16[1,240,1536]{2,1,0:T(8,128)(2,1)} %get-tuple-element.19), channel_id=1, source_target_pairs={{0,1},{1,2},{2,3},{3,4},{4,5},{5,6},{6,7},{7,8},{8,9},{9,10},{10,1... | collective-permute-start | bytes 2211848 | tf_op jit(solution)/shard_map/ppermute | solution.py:304
  31.9 7.2 %copy-start.1 = (bf16[16,48,384]{2,1,0:T(8,128)(2,1)}, bf16[16,48,384]{2,1,0:T(8,128)(2,1)S(1)}, u32[]{:S(2)}) copy-start(bf16[16,48,384]{2,1,0:T(8,128)(2,1)S(1)} %all-to-all-done) | copy-start | bytes 1769476
  31.9 31.9 %all-to-all-start.1 = ((bf16[16,48,512]{2,1,0:T(8,128)(2,1)}), bf16[16,48,512]{2,1,0:T(8,128)(2,1)S(1)}, u32[]{:S(2)}, u32[]{:S(2)}) async-start(bf16[16,48,512]{2,1,0:T(8,128)(2,1)} %get-tuple-element.16), calls=%async_computation.1 | async-start | bytes 1572864 | tf_op jit(solution)/shard_map/all_to_all | solution.py:285
  36.5 27.2 %collective-permute-start = (bf16[1,240,1536]{2,1,0:T(8,128)(2,1)}, bf16[1,240,1536]{2,1,0:T(8,128)(2,1)S(1)}, u32[]{:S(2)}, u32[]{:S(2)}) collective-permute-start(bf16[1,240,1536]{2,1,0:T(8,128)(2,1)} %get-tuple-element.20), channel_id=1, source_target_pairs={{1,0},{2,1},{3,2},{4,3},{5,4},{6,5},{7,6},{8,7},{9,8},{10,9},{11,1... | collective-permute-start | bytes 2211848 | tf_op jit(solution)/shard_map/ppermute | solution.py:304
  39.0 0.9 copy-start.2
  63.7 0.9 copy-start.3
  63.7 1.1 %copy-start = (bf16[16,48,512]{2,1,0:T(8,128)(2,1)}, bf16[16,48,512]{2,1,0:T(8,128)(2,1)S(1)}, u32[]{:S(2)}) copy-start(bf16[16,48,512]{2,1,0:T(8,128)(2,1)S(1)} %all-to-all-done.1) | copy-start | bytes 2359300

commit v3 on v2

--- a/solution.py
+++ b/solution.py
@@ -292,9 +292,9 @@
     devices = lax.axis_size("lat")
     up = [(i, i + 1) for i in range(devices - 1)]
     down = [(j, i) for i, j in up]
-    per_step = divisor(rows, 6)
+    per_step = divisor(rows, 4)
     blocks = rows // per_step
-    counts = [blocks] if blocks < 4 else [blocks * 3 // 8, blocks - blocks * 3 // 8]
+    counts = [blocks] if blocks < 4 else [blocks * 5 // 12, blocks - blocks * 5 // 12]
     firsts = [per_step * sum(counts[:i]) for i in range(len(counts))]
     windows = []
     for start, count in zip(firsts, counts):

time: 94.6 us -> 93 us (0.983)
  waiting for transfers between devices: 4.49 us -> 3.42 us
    ppermute x1, waiting for transfers between devices: 4.01 us -> 2.94 us  [shards(): lax.ppermute(q[:1], 'lat', down)]
  transfers between devices with their start and end apart: 4 -> 4, of which waited for: 2 -> 2; matrix products, arithmetic and copies ran while one was open for 4% -> 4% of each run, Pallas kernels for 29% -> 31%
where the time goes in v3:
time: 93 us; the launch traced here: 92.5 us
  Pallas kernels  66.1 us (71%)
  starting transfers between devices  17 us (18%)
  local copies, waits for them, and re-layouts  5.89 us (6%)
  waiting for transfers between devices  3.42 us (4%)
    pallas_call x2, Pallas kernels, advect(): pl.pallas_call(functools.partial(advect_kernel, levels, first, begin, end...  48.5 us
    all_to_all x2, starting transfers between devices, exchange(): lax.all_to_all(value, 'lat', split_axis=0, concat_axis=0, tiled=True)  11.2 us
    pallas_call x1, Pallas kernels, legendre_synthesis(): pl.pallas_call(functools.partial(legendre_kernel, windows, rows), grid=(w...  9.98 us
    pallas_call x1, Pallas kernels, tables(): pl.pallas_call(functools.partial(tables_kernel, waves, wave_total), out_s...  7.59 us
    unnamed x9, local copies, waits for them, and re-layouts  3.35 us
    ppermute x1, starting transfers between devices, shards(): lax.ppermute(q[-1:], 'lat', up)  3.33 us
    ppermute x1, waiting for transfers between devices, shards(): lax.ppermute(q[:1], 'lat', down)  2.94 us
    slice x1, local copies, waits for them, and re-layouts, shards(): q[-1:]  2.55 us
  transfers between devices with their start and end apart: 4, of which 2 were waited for; matrix products, arithmetic and copies ran while one was open for 4% of the time, Pallas kernels for 31%

profile of v3, /device:TPU:13, one launch (start us, length us, event | category | flops | bytes accessed | tf_op | source)
XLA Modules:
  0.0 92.5 jit_solution(2664216721971519757)
XLA Ops:
  0.0 10.0 %legendre.1 = (bf16[16,48,384]{2,1,0:T(8,128)(2,1)}, bf16[16,48,512]{2,1,0:T(8,128)(2,1)}) custom-call(s32[1]{0:T(128)} %bitcast.first_ref, bf16[24,2,2,8,384]{4,3,2,1,0:T(8,128)(2,1)} %spec_ref.1, bf16[24,384,768]{2,1,0:T(8,128)(2,1)} %leg_ref.1), custom_call_target="tpu_custom_call" | custom-call | flops 452984832 | bytes 15335424 | tf_op jit(solution)/shard_map/legendre/pallas_call | solution.py:68
  10.0 6.6 %all-to-all-start = ((bf16[16,48,384]{2,1,0:T(8,128)(2,1)}), bf16[16,48,384]{2,1,0:T(8,128)(2,1)S(1)}, u32[]{:S(2)}, u32[]{:S(2)}) async-start(bf16[16,48,384]{2,1,0:T(8,128)(2,1)} %get-tuple-element.12), calls=%async_computation | async-start | bytes 1179648 | tf_op jit(solution)/shard_map/all_to_all | solution.py:285
  16.5 2.5 %slice_bitcast_fusion = (bf16[1,240,1536]{2,1,0:T(8,128)(2,1)}, bf16[1,240,1536]{2,1,0:T(8,128)(2,1)}) fusion(bf16[48,30,8,1536]{3,2,1,0:T(8,128)(2,1)} %param.7), kind=kLoop, calls=%fused_computation | loop fusion | bytes 2949120 | tf_op jit(solution)/shard_map/slice | solution.py:304
  19.1 3.3 %collective-permute-start.1 = (bf16[1,240,1536]{2,1,0:T(8,128)(2,1)}, bf16[1,240,1536]{2,1,0:T(8,128)(2,1)S(1)}, u32[]{:S(2)}, u32[]{:S(2)}) collective-permute-start(bf16[1,240,1536]{2,1,0:T(8,128)(2,1)} %get-tuple-element.19), channel_id=1, source_target_pairs={{0,1},{1,2},{2,3},{3,4},{4,5},{5,6},{6,7},{7,8},{8,9},{9,10},{10,1... | collective-permute-start | bytes 2211848 | tf_op jit(solution)/shard_map/ppermute | solution.py:304
  22.4 1.4 %copy.7.decay_ref = f32[30,8]{1,0:T(8,128)} copy(f32[30,8]{0,1:T(8,128)} %param.9) | data formatting | bytes 1920 | tf_op args[4]
  23.8 7.6 %tables.1 = (bf16[768,1536]{1,0:T(8,128)(2,1)}, bf16[2,240,240]{2,1,0:T(8,128)(2,1)}) custom-call(f32[30,30]{1,0:T(8,128)} %rates_ref.1, f32[30,8]{1,0:T(8,128)} %copy.7.decay_ref), custom_call_target="tpu_custom_call" | custom-call | flops 47185920 | bytes 2359296 | tf_op jit(solution)/shard_map/tables/pallas_call | solution.py:141
  31.4 0.5 all-to-all-done
  31.9 0.0 copy-start.1
  31.9 4.7 %all-to-all-start.1 = ((bf16[16,48,512]{2,1,0:T(8,128)(2,1)}), bf16[16,48,512]{2,1,0:T(8,128)(2,1)S(1)}, u32[]{:S(2)}, u32[]{:S(2)}) async-start(bf16[16,48,512]{2,1,0:T(8,128)(2,1)} %get-tuple-element.16), calls=%async_computation.1 | async-start | bytes 1572864 | tf_op jit(solution)/shard_map/all_to_all | solution.py:285
  36.5 2.4 %collective-permute-start = (bf16[1,240,1536]{2,1,0:T(8,128)(2,1)}, bf16[1,240,1536]{2,1,0:T(8,128)(2,1)S(1)}, u32[]{:S(2)}, u32[]{:S(2)}) collective-permute-start(bf16[1,240,1536]{2,1,0:T(8,128)(2,1)} %get-tuple-element.20), channel_id=1, source_target_pairs={{1,0},{2,1},{3,2},{4,3},{5,4},{6,5},{7,6},{8,7},{9,8},{10,9},{11,1... | collective-permute-start | bytes 2211848 | tf_op jit(solution)/shard_map/ppermute | solution.py:304
  39.0 0.0 collective-permute-done.1.prev_ref
  39.0 0.0 copy-start.2
  39.0 0.0 copy-done.1
  39.0 0.9 copy-done.2
  39.9 20.9 %advect.2.refs_3_ = bf16[48,240,1536]{2,1,0:T(8,128)(2,1)} custom-call(bf16[2,240,240]{2,1,0:T(8,128)(2,1)} %get-tuple-element.15.weight_ref, bf16[48,240,1536]{2,1,0:T(8,128)(2,1)} %bitcast.9, bf16[48,240,1536]{2,1,0:T(8,128)(2,1)} %bitcast.10, bf16[1,240,1536]{2,1,0:T(8,128)(2,1)} %copy-done.2, bf16[768,384]{1,0:T(8,128)(2,1)} %bitcast.15, ...), custom_call_target="tpu_custom_call" | custom-call | flops 10616832000 | bytes 36864000 | tf_op jit(solution)/shard_map/advect/pallas_call | solution.py:264
  60.8 2.9 %collective-permute-done.refs_0_ = bf16[1,240,1536]{2,1,0:T(8,128)(2,1)S(1)} collective-permute-done((bf16[1,240,1536]{2,1,0:T(8,128)(2,1)}, bf16[1,240,1536]{2,1,0:T(8,128)(2,1)S(1)}, u32[]{:S(2)}, u32[]{:S(2)}) %collective-permute-start) | collective-permute-done | bytes 737312 | tf_op jit(solution)/shard_map/ppermute | solution.py:304
  63.7 0.0 copy-start.3
  63.7 0.0 all-to-all-done.1
  63.7 0.0 copy-start
  63.7 0.9 copy-done.3
  64.6 0.2 copy-done
  64.9 27.6 %advect.3 = bf16[48,240,1536]{2,1,0:T(8,128)(2,1)} custom-call(bf16[2,240,240]{2,1,0:T(8,128)(2,1)} %get-tuple-element.15.weight_ref, bf16[48,240,1536]{2,1,0:T(8,128)(2,1)} %bitcast.11, bf16[48,240,1536]{2,1,0:T(8,128)(2,1)} %bitcast.12, bf16[48,240,1536]{2,1,0:T(8,128)(2,1)} %bitcast.13, ...), custom_call_target="tpu_custom_call", output_to_operand_aliasing={{}: (7, {})} | custom-call | flops 14863564800 | bytes 51609600 | tf_op jit(solution)/shard_map/advect/pallas_call | solution.py:264
Async XLA Ops:
  10.0 21.9 %all-to-all-start = ((bf16[16,48,384]{2,1,0:T(8,128)(2,1)}), bf16[16,48,384]{2,1,0:T(8,128)(2,1)S(1)}, u32[]{:S(2)}, u32[]{:S(2)}) async-start(bf16[16,48,384]{2,1,0:T(8,128)(2,1)} %get-tuple-element.12), calls=%async_computation | async-start | bytes 1179648 | tf_op jit(solution)/shard_map/all_to_all | solution.py:285
  19.1 19.9 %collective-permute-start.1 = (bf16[1,240,1536]{2,1,0:T(8,128)(2,1)}, bf16[1,240,1536]{2,1,0:T(8,128)(2,1)S(1)}, u32[]{:S(2)}, u32[]{:S(2)}) collective-permute-start(bf16[1,240,1536]{2,1,0:T(8,128)(2,1)} %get-tuple-element.19), channel_id=1, source_target_pairs={{0,1},{1,2},{2,3},{3,4},{4,5},{5,6},{6,7},{7,8},{8,9},{9,10},{10,1... | collective-permute-start | bytes 2211848 | tf_op jit(solution)/shard_map/ppermute | solution.py:304
  31.9 7.2 %copy-start.1 = (bf16[16,48,384]{2,1,0:T(8,128)(2,1)}, bf16[16,48,384]{2,1,0:T(8,128)(2,1)S(1)}, u32[]{:S(2)}) copy-start(bf16[16,48,384]{2,1,0:T(8,128)(2,1)S(1)} %all-to-all-done) | copy-start | bytes 1769476
  31.9 31.9 %all-to-all-start.1 = ((bf16[16,48,512]{2,1,0:T(8,128)(2,1)}), bf16[16,48,512]{2,1,0:T(8,128)(2,1)S(1)}, u32[]{:S(2)}, u32[]{:S(2)}) async-start(bf16[16,48,512]{2,1,0:T(8,128)(2,1)} %get-tuple-element.16), calls=%async_computation.1 | async-start | bytes 1572864 | tf_op jit(solution)/shard_map/all_to_all | solution.py:285
  36.5 27.2 %collective-permute-start = (bf16[1,240,1536]{2,1,0:T(8,128)(2,1)}, bf16[1,240,1536]{2,1,0:T(8,128)(2,1)S(1)}, u32[]{:S(2)}, u32[]{:S(2)}) collective-permute-start(bf16[1,240,1536]{2,1,0:T(8,128)(2,1)} %get-tuple-element.20), channel_id=1, source_target_pairs={{1,0},{2,1},{3,2},{4,3},{5,4},{6,5},{7,6},{8,7},{9,8},{10,9},{11,1... | collective-permute-start | bytes 2211848 | tf_op jit(solution)/shard_map/ppermute | solution.py:304
  39.0 0.9 copy-start.2
  63.7 0.9 copy-start.3
  63.7 1.1 %copy-start = (bf16[16,48,512]{2,1,0:T(8,128)(2,1)}, bf16[16,48,512]{2,1,0:T(8,128)(2,1)S(1)}, u32[]{:S(2)}) copy-start(bf16[16,48,512]{2,1,0:T(8,128)(2,1)S(1)} %all-to-all-done.1) | copy-start | bytes 2359300
